TPU v7x, 512 devices: a whole 4x8x8 slice. The times are simulated.
512 devices in a mesh: grp: 8 (over z_hi, x), gx: 8 (over z_lo, core), gy: 8 (over y).
Axes of the slice: x: 4, y: 8, z: 8 (z_hi: 2, z_lo: 4; z = z_hi * 4 + z_lo), core: 2. Of those that a mesh axis runs over, the one named last changes fastest.
Arguments:
- efield: float32 [8, 3, 128, 128, 128], P('grp', None, 'gx', 'gy'), may hold values from -6 to 6
- hfield: float32 [8, 3, 128, 128, 128], P('grp', None, 'gx', 'gy'), may hold values from -6 to 6
- fwd_dft: bfloat16 [8, 2, 2, 3, 128, 128, 128], P('grp', None, None, None, 'gx', 'gy'), may hold values from -6 to 6
- adj_dft: bfloat16 [8, 2, 2, 3, 128, 128, 128], P('grp', None, None, None, 'gx', 'gy'), may hold values from -6 to 6
- permittivity: float32 [128, 128, 128], P('gx', 'gy'), may hold values from 1 to 4
- source_amp: float32 [8, 128, 128], P('grp', 'gx', 'gy'), may hold values from -6 to 6
- source_plane: int32 [8], P('grp'), may hold values from 4 to 123
- freqs: float32 [8, 2], P('grp'), may hold values from 0.2 to 1.5
- pml_width: int32 [2], replicated, may hold values from 2 to 7
- design_blocks: int32 [128], replicated, may hold values from 0 to 255, as said below
Outputs:
- grad_step: float32 [2, 128, 128, 128], P(None, 'gx', 'gy')
Inputs may be any that keep to these rules, and one draw needn't show every extreme that they name: `design_blocks`: distinct block numbers.
All inputs are finite; a program needn't handle non-finite values.
Results may differ from a plain program's by a relative error of at most 0.0003.
Values sent between devices are 32-bit elements; how exact they have to be, the bound alone decides.
A program may use at most 64 MiB of HBM per device.

v0:
```python
import jax
import jax.numpy as jnp
from jax import lax
from jax.sharding import PartitionSpec as P

BS = 8
STEPS = 2
courant = 0.5
absorb = 0.8


def shifted(value, axis, steps):
    count = lax.axis_size(axis)
    leading, last = (max(0, -steps), min(count, count - steps))
    return lax.ppermute(value, axis, [(source, source + steps) for source in range(leading, last)])


def ahead_z(field):
    zero = jnp.zeros_like(field[:, :, :1])
    return jnp.concatenate([field[:, :, 1:], zero], 2) - field


def behind_z(field):
    zero = jnp.zeros_like(field[:, :, :1])
    return field - jnp.concatenate([zero, field[:, :, :-1]], 2)


def profile(cells, count, width):
    place = cells.astype(jnp.float32)
    dist = jnp.minimum(place, count - 1.0 - place)
    wide = width.astype(jnp.float32)
    return jnp.maximum(0.0, (wide - dist) / wide) ** 2


def update_magnetic(fields_e, fields_h, damp):
    ex, ey, ez = fields_e
    hx, hy, hz = fields_h
    rim_x = shifted(jnp.stack([ey[0], ez[0]]), "gx", -1)
    rim_y = shifted(jnp.stack([ex[:, 0], ez[:, 0]]), "gy", -1)
    ey_dx = jnp.concatenate([ey[1:], rim_x[0][None]], 0) - ey
    ez_dx = jnp.concatenate([ez[1:], rim_x[1][None]], 0) - ez
    ex_dy = jnp.concatenate([ex[:, 1:], rim_y[0][:, None]], 1) - ex
    ez_dy = jnp.concatenate([ez[:, 1:], rim_y[1][:, None]], 1) - ez
    hx = damp * (hx - courant * (ez_dy - ahead_z(ey)))
    hy = damp * (hy - courant * (ahead_z(ex) - ez_dx))
    hz = damp * (hz - courant * (ey_dx - ex_dy))
    return (hx, hy, hz)


def update_electric(fields_e, fields_h, damp, coef, drive):
    ex, ey, ez = fields_e
    hx, hy, hz = fields_h
    last_x = hx.shape[0] - 1
    last_y = hx.shape[1] - 1
    rim_x = shifted(jnp.stack([hy[last_x], hz[last_x]]), "gx", 1)
    rim_y = shifted(jnp.stack([hx[:, last_y], hz[:, last_y]]), "gy", 1)
    hy_dx = hy - jnp.concatenate([rim_x[0][None], hy[:-1]], 0)
    hz_dx = hz - jnp.concatenate([rim_x[1][None], hz[:-1]], 0)
    hx_dy = hx - jnp.concatenate([rim_y[0][:, None], hx[:, :-1]], 1)
    hz_dy = hz - jnp.concatenate([rim_y[1][:, None], hz[:, :-1]], 1)
    ex = damp * (ex + coef * (hz_dy - behind_z(hy)))
    ey = damp * (ey + coef * (behind_z(hx) - hz_dx))
    ez = damp * (ez + coef * (hy_dx - hx_dy) + drive)
    return (ex, ey, ez)


def body(
    efield,
    hfield,
    fwd_dft,
    adj_dft,
    permittivity,
    source_amp,
    source_plane,
    freqs,
    pml_width,
    design_blocks,
):
    cells_x, cells_y, cells_z = permittivity.shape
    total_x = cells_x * lax.axis_size("gx")
    total_y = cells_y * lax.axis_size("gy")
    global_x = lax.axis_index("gx") * cells_x + jnp.arange(cells_x, dtype=jnp.int32)
    global_y = lax.axis_index("gy") * cells_y + jnp.arange(cells_y, dtype=jnp.int32)
    plane = (jnp.arange(cells_z, dtype=jnp.int32) == source_plane[0]).astype(jnp.float32)
    shaped = source_amp[0][:, :, None] * plane[None, None, :]
    omega = freqs[0]
    acc = adj_dft[0].astype(jnp.float32)
    damp = jnp.exp(
        -absorb
        * (
            profile(global_x, total_x, pml_width[0])[:, None]
            + profile(global_y, total_y, pml_width[1])[None, :]
        )
    )[:, :, None]
    coef = courant / permittivity
    fields_e = (efield[0, 0], efield[0, 1], efield[0, 2])
    fields_h = (hfield[0, 0], hfield[0, 1], hfield[0, 2])
    for step in range(STEPS):
        tval = jnp.float32(step + 1)
        fields_h = update_magnetic(fields_e, fields_h, damp)
        fields_e = update_electric(
            fields_e, fields_h, damp, coef, shaped * jnp.sin(omega[0] * tval)
        )
        efull = jnp.stack(fields_e)
        cosv = jnp.cos(omega * tval)[:, None, None, None, None]
        sinv = jnp.sin(omega * tval)[:, None, None, None, None]
        acc = jnp.stack([acc[:, 0] + cosv * efull, acc[:, 1] - sinv * efull], axis=1)
    cell_id = (global_x // BS)[:, None] * (total_y // BS) + (global_y // BS)[None, :]
    mask = jnp.any(design_blocks[:, None, None] == cell_id[None], axis=0).astype(jnp.float32)[
        :, :, None
    ]
    term = jnp.sum(fwd_dft[0].astype(jnp.float32) * acc, axis=(1, 2)) * mask[None]
    count = jnp.float32(design_blocks.shape[0] * BS * BS * cells_z)
    grad = lax.psum(term, "grp")
    squares = lax.psum(jnp.sum(grad * grad, axis=(1, 2, 3)), ("gx", "gy"))
    return grad / jnp.sqrt(squares / count + 1e-05)[:, None, None, None]


def solution(mesh):
    in_specs = (
        P("grp", None, "gx", "gy", None),
        P("grp", None, "gx", "gy", None),
        P("grp", None, None, None, "gx", "gy", None),
        P("grp", None, None, None, "gx", "gy", None),
        P("gx", "gy", None),
        P("grp", "gx", "gy"),
        P("grp"),
        P("grp", None),
        P(),
        P(),
    )
    out_specs = P(None, "gx", "gy", None)
    return jax.shard_map(body, mesh=mesh, in_specs=in_specs, out_specs=out_specs, check_vma=False)
```

profile of v0, /device:TPU:8, one launch (start us, length us, event | category | flops | bytes accessed | tf_op | source)
XLA Modules:
  0.0 310.4 jit_solution(465055666218704547)
XLA Ops:
  6.5 1.1 slice_bitcast_fusion.1
  7.7 0.0 copy-start.7
  7.7 7.7 %collective-permute-start.1 = (f32[2,16,128]{2,1,0:T(8,128)S(1)}, f32[2,16,128]{2,1,0:T(8,128)S(1)}, u32[]{:S(2)}, u32[]{:S(2)}) collective-permute-start(f32[2,16,128]{2,1,0:T(8,128)S(1)} %pad_maximum_fusion.3), channel_id=1, source_target_pairs={{1,0},{2,1},{3,2},{4,3},{5,4},{6,5},{7,6},{9,8},{10,9},{11,10},{12... | collective-permute-start | bytes 49160 | tf_op jit(solution)/shard_map/ppermute | solution.py:15
  15.5 0.7 slice_bitcast_fusion.6
  16.2 1.3 collective-permute-start
  17.5 1.0 slice_bitcast_fusion.4
  18.5 1.4 fusion.73
  21.9 0.7 cosine_bitcast_fusion.1
  22.6 0.0 copy-start.6
  22.6 0.0 copy-start
  22.6 0.0 copy-start.4
  22.6 0.1 bitcast_convert_fusion
  22.8 0.1 multiply_exponential_fusion
  22.9 0.1 broadcast_add_fusion
  23.0 0.4 compare_reduce_fusion
  23.5 0.1 slice.303
  23.6 0.1 slice.298
  23.7 0.0 copy-start.1
  23.7 0.0 copy-start.5
  23.9 0.0 collective-permute-done.1
  24.0 0.1 fusion.15
  24.2 0.1 fusion.23
  24.3 3.0 collective-permute-start.3
  27.4 1.9 collective-permute-start.2
  29.4 3.7 %collective-permute-done.2 = f32[2,16,128]{2,1,0:T(8,128)S(1)} collective-permute-done((f32[2,16,128]{2,1,0:T(8,128)S(1)}, f32[2,16,128]{2,1,0:T(8,128)S(1)}, u32[]{:S(2)}, u32[]{:S(2)}) %collective-permute-start.2) | collective-permute-done | bytes 16416 | tf_op jit(solution)/shard_map/ppermute | solution.py:15
  33.0 0.2 fusion.19
  33.3 0.1 fusion.27
  33.5 1.3 collective-permute-start.4
  34.8 0.1 slice.325
  35.0 0.1 slice.330
  35.1 1.9 collective-permute-start.5
  37.0 3.7 %collective-permute-done.5 = f32[2,16,128]{2,1,0:T(8,128)S(1)} collective-permute-done((f32[2,16,128]{2,1,0:T(8,128)S(1)}, f32[2,16,128]{2,1,0:T(8,128)S(1)}, u32[]{:S(2)}, u32[]{:S(2)}) %collective-permute-start.5) | collective-permute-done | bytes 16416 | tf_op jit(solution)/shard_map/ppermute | solution.py:15
  40.7 0.2 fusion.38
  41.0 2.0 collective-permute-start.7
  43.1 1.9 collective-permute-start.6
  45.0 0.1 fusion.52
  45.2 3.6 %collective-permute-done.6 = f32[2,16,128]{2,1,0:T(8,128)S(1)} collective-permute-done((f32[2,16,128]{2,1,0:T(8,128)S(1)}, f32[2,16,128]{2,1,0:T(8,128)S(1)}, u32[]{:S(2)}, u32[]{:S(2)}) %collective-permute-start.6) | collective-permute-done | bytes 16416 | tf_op jit(solution)/shard_map/ppermute | solution.py:15
  48.7 0.2 fusion.43
  49.0 0.0 copy-start.3
  49.0 0.3 fusion.2
  49.3 0.8 copy-done.3
  50.1 0.2 fusion
  50.3 0.8 broadcast_multiply_fusion
  51.1 0.0 all-reduce.10.cloned.1.call-update
  51.1 115.3 %all-reduce.10.cloned.1.call-done = f32[2,16,16,128]{3,2,1,0:T(8,128)} async-done(((f32[2,16,16,128]{3,2,1,0:T(8,128)}), f32[2,16,16,128]{3,2,1,0:T(8,128)}) %all-reduce.10.cloned.1.call-update) | async-done | bytes 262160 | tf_op jit(solution)/shard_map/psum | solution.py:114
  166.4 1.1 multiply_reduce_fusion
  167.5 134.2 %psum.15 = f32[2]{0:T(128)S(1)} all-reduce(f32[2]{0:T(128)S(1)} %multiply_reduce_fusion), channel_id=1, replica_groups=mesh['grp'=8,'gx'=8,'gy'=8] {'gx','gy'}, use_global_device_ids=true, to_apply=%region_4.5 | all-reduce | flops 2 | bytes 16 | tf_op jit(solution)/shard_map/psum | solution.py:115
  301.8 1.7 broadcast_divide_fusion
  (60 shorter events, 0.4 us)
Async XLA Ops:
  6.5 16.0 %copy-start.2 = (bf16[1,2,2,3,16,16,128]{6,5,4,3,2,1,0:T(8,128)(2,1)S(1)}, bf16[1,2,2,3,16,16,128]{6,5,4,3,2,1,0:T(8,128)(2,1)}, u32[]{:S(2)}) copy-start(bf16[1,2,2,3,16,16,128]{6,5,4,3,2,1,0:T(8,128)(2,1)} %param.13) | copy-start | bytes 2359300
  6.5 159.9 %all-reduce.10.cloned.1.call-start = ((), (), s32[]{:S(2)}) async-start(), calls=%async_computation | async-start | bytes 524288 | tf_op jit(solution)/shard_map/psum | solution.py:114
  7.7 15.3 %copy-start.7 = (s32[128]{0:T(128)S(1)}, s32[128]{0:T(128)}, u32[]{:S(2)}) copy-start(s32[128]{0:T(128)} %param.19) | copy-start | bytes 1540
  7.7 16.2 %collective-permute-start.1 = (f32[2,16,128]{2,1,0:T(8,128)S(1)}, f32[2,16,128]{2,1,0:T(8,128)S(1)}, u32[]{:S(2)}, u32[]{:S(2)}) collective-permute-start(f32[2,16,128]{2,1,0:T(8,128)S(1)} %pad_maximum_fusion.3), channel_id=1, source_target_pairs={{1,0},{2,1},{3,2},{4,3},{5,4},{6,5},{7,6},{9,8},{10,9},{11,10},{12... | collective-permute-start | bytes 49160 | tf_op jit(solution)/shard_map/ppermute | solution.py:15
  16.2 7.8 %collective-permute-start = (f32[2,16,128]{2,1,0:T(8,128)S(1)}, f32[2,16,128]{2,1,0:T(8,128)S(1)}, u32[]{:S(2)}, u32[]{:S(2)}) collective-permute-start(f32[2,16,128]{2,1,0:T(8,128)S(1)} %pad_maximum_fusion.2), channel_id=1, source_target_pairs={{8,0},{16,8},{24,16},{32,24},{40,32},{48,40},{56,48},{9,1},{17,9},... | collective-permute-start | bytes 49160 | tf_op jit(solution)/shard_map/ppermute | solution.py:15
  22.6 1.1 copy-start.6
  22.6 1.4 copy-start
  22.6 1.4 copy-start.4
  23.7 9.4 %copy-start.1 = (f32[16,16,128]{2,1,0:T(8,128)S(1)}, f32[16,16,128]{2,1,0:T(8,128)}, u32[]{:S(2)}) copy-start(f32[16,16,128]{2,1,0:T(8,128)} %param.14) | copy-start | bytes 393220
  23.7 9.4 %copy-start.5 = (f32[1,16,16]{2,1,0:T(8,128)S(1)}, f32[1,16,16]{2,1,0:T(8,128)}, u32[]{:S(2)}) copy-start(f32[1,16,16]{2,1,0:T(8,128)} %param.15) | copy-start | bytes 3076
  24.3 5.0 %collective-permute-start.3 = (f32[2,16,128]{2,1,0:T(8,128)S(1)}, f32[2,16,128]{2,1,0:T(8,128)S(1)}, u32[]{:S(2)}, u32[]{:S(2)}) collective-permute-start(f32[2,16,128]{2,1,0:T(8,128)S(1)} %pad_maximum_fusion.5), channel_id=1, source_target_pairs={{0,8},{8,16},{16,24},{24,32},{32,40},{40,48},{48,56},{1,9},{9,17},... | collective-permute-start | bytes 49160 | tf_op jit(solution)/shard_map/ppermute | solution.py:15
  27.4 5.6 %collective-permute-start.2 = (f32[2,16,128]{2,1,0:T(8,128)S(1)}, f32[2,16,128]{2,1,0:T(8,128)S(1)}, u32[]{:S(2)}, u32[]{:S(2)}) collective-permute-start(f32[2,16,128]{2,1,0:T(8,128)S(1)} %pad_maximum_fusion.4), channel_id=1, source_target_pairs={{0,1},{1,2},{2,3},{3,4},{4,5},{5,6},{6,7},{8,9},{9,10},{10,11},{11... | collective-permute-start | bytes 49160 | tf_op jit(solution)/shard_map/ppermute | solution.py:15
  33.5 3.6 %collective-permute-start.4 = (f32[2,16,128]{2,1,0:T(8,128)S(1)}, f32[2,16,128]{2,1,0:T(8,128)S(1)}, u32[]{:S(2)}, u32[]{:S(2)}) collective-permute-start(f32[2,16,128]{2,1,0:T(8,128)S(1)} %pad_maximum_fusion.6), channel_id=1, source_target_pairs={{8,0},{16,8},{24,16},{32,24},{40,32},{48,40},{56,48},{9,1},{17,9},... | collective-permute-start | bytes 49160 | tf_op jit(solution)/shard_map/ppermute | solution.py:15
  35.1 5.6 %collective-permute-start.5 = (f32[2,16,128]{2,1,0:T(8,128)S(1)}, f32[2,16,128]{2,1,0:T(8,128)S(1)}, u32[]{:S(2)}, u32[]{:S(2)}) collective-permute-start(f32[2,16,128]{2,1,0:T(8,128)S(1)} %pad_maximum_fusion.7), channel_id=1, source_target_pairs={{1,0},{2,1},{3,2},{4,3},{5,4},{6,5},{7,6},{9,8},{10,9},{11,10},{12... | collective-permute-start | bytes 49160 | tf_op jit(solution)/shard_map/ppermute | solution.py:15
  41.0 4.0 %collective-permute-start.7 = (f32[2,16,128]{2,1,0:T(8,128)S(1)}, f32[2,16,128]{2,1,0:T(8,128)S(1)}, u32[]{:S(2)}, u32[]{:S(2)}) collective-permute-start(f32[2,16,128]{2,1,0:T(8,128)S(1)} %pad_maximum_fusion.9), channel_id=1, source_target_pairs={{0,8},{8,16},{16,24},{24,32},{32,40},{40,48},{48,56},{1,9},{9,17},... | collective-permute-start | bytes 49160 | tf_op jit(solution)/shard_map/ppermute | solution.py:15
  43.1 5.7 %collective-permute-start.6 = (f32[2,16,128]{2,1,0:T(8,128)S(1)}, f32[2,16,128]{2,1,0:T(8,128)S(1)}, u32[]{:S(2)}, u32[]{:S(2)}) collective-permute-start(f32[2,16,128]{2,1,0:T(8,128)S(1)} %pad_maximum_fusion.8), channel_id=1, source_target_pairs={{0,1},{1,2},{2,3},{3,4},{4,5},{5,6},{6,7},{8,9},{9,10},{10,11},{11... | collective-permute-start | bytes 49160 | tf_op jit(solution)/shard_map/ppermute | solution.py:15
  49.0 1.1 copy-start.3
Sparse Core Ops, SparseCore 0:
  51.3 115.1 all-reduce.9
where the time goes:
time: 311 us; the launch traced here: 310 us
  blocking collectives  134 us (43%)
  waiting for transfers between devices  126 us (41%)
  starting transfers between devices  21.1 us (7%)
  between operations  16.2 us (5%)
  other arithmetic  6.79 us (2%)
  local copies, waits for them, and re-layouts  5.7 us (2%)
    psum x1, blocking collectives, body(): squares = lax.psum(jnp.sum(grad * grad, axis=(1, 2, 3)), ('gx', 'gy'))  134 us
    psum x1, waiting for transfers between devices, body(): grad = lax.psum(term, 'grp')  115 us
    ppermute x8, starting transfers between devices, shifted(): lax.ppermute(value, axis, [(source, source + steps) for source in range(l...  21.1 us
    ppermute x8, waiting for transfers between devices, shifted(): lax.ppermute(value, axis, [(source, source + steps) for source in range(l...  11 us
  transfers between devices with their start and end apart: 9, of which 4 were waited for; matrix products, arithmetic and copies ran while one was open for 2% of the time, Pallas kernels for 0%

commit v1 on v0

--- a/solution.py
+++ b/solution.py
@@ -111,7 +111,7 @@
     ]
     term = jnp.sum(fwd_dft[0].astype(jnp.float32) * acc, axis=(1, 2)) * mask[None]
     count = jnp.float32(design_blocks.shape[0] * BS * BS * cells_z)
-    grad = lax.psum(term, "grp")
+    grad = jnp.sum(lax.all_gather(term, "grp"), axis=0)
     squares = lax.psum(jnp.sum(grad * grad, axis=(1, 2, 3)), ("gx", "gy"))
     return grad / jnp.sqrt(squares / count + 1e-05)[:, None, None, None]
 

time: 311 us -> 281 us (0.904)
  the two profiles are of different devices: /device:TPU:8 before, /device:TPU:2 now
where the time goes in v1:
time: 281 us; the launch traced here: 280 us
  blocking collectives  135 us (48%)
  waiting for transfers between devices  97.8 us (35%)
  starting transfers between devices  18.9 us (7%)
  between operations  16.2 us (6%)
  other arithmetic  6.58 us (2%)
  local copies, waits for them, and re-layouts  5.7 us (2%)
    psum x1, blocking collectives, body(): squares = lax.psum(jnp.sum(grad * grad, axis=(1, 2, 3)), ('gx', 'gy'))  135 us
    all_gather x1, waiting for transfers between devices, body(): grad = jnp.sum(lax.all_gather(term, 'grp'), axis=0)  90.5 us
    ppermute x8, starting transfers between devices, shifted(): lax.ppermute(value, axis, [(source, source + steps) for source in range(l...  18.9 us
    ppermute x8, waiting for transfers between devices, shifted(): lax.ppermute(value, axis, [(source, source + steps) for source in range(l...  7.29 us
  transfers between devices with their start and end apart: 9, of which 5 were waited for; matrix products, arithmetic and copies ran while one was open for 2% of the time, Pallas kernels for 0%

profile of v1, /device:TPU:2, one launch (start us, length us, event | category | flops | bytes accessed | tf_op | source)
XLA Modules:
  0.0 280.0 jit_solution(8659843185707431241)
XLA Ops:
  6.5 1.1 slice_bitcast_fusion.1
  7.7 0.0 copy-start.7
  7.7 1.3 collective-permute-start.1
  9.0 0.7 slice_bitcast_fusion.6
  9.7 1.3 collective-permute-start
  11.0 1.0 slice_bitcast_fusion.4
  12.0 1.4 fusion.73
  15.4 0.7 cosine_bitcast_fusion.1
  16.1 0.0 copy-start.6
  16.1 0.0 copy-start
  16.2 0.0 copy-start.4
  16.2 0.1 bitcast_convert_fusion
  16.4 0.1 multiply_exponential_fusion
  16.4 0.1 broadcast_add_fusion
  16.5 0.4 compare_reduce_fusion
  17.0 0.1 slice.303
  17.1 0.1 slice.298
  17.2 0.0 copy-start.5
  17.5 0.1 fusion.15
  17.7 0.1 fusion.23
  17.8 3.0 %collective-permute-start.3 = (f32[2,16,128]{2,1,0:T(8,128)S(1)}, f32[2,16,128]{2,1,0:T(8,128)S(1)}, u32[]{:S(2)}, u32[]{:S(2)}) collective-permute-start(f32[2,16,128]{2,1,0:T(8,128)S(1)} %pad_maximum_fusion.5), channel_id=1, source_target_pairs={{0,8},{8,16},{16,24},{24,32},{32,40},{40,48},{48,56},{1,9},{9,17},... | collective-permute-start | bytes 49160 | tf_op jit(solution)/shard_map/ppermute | solution.py:15
  20.9 4.5 %collective-permute-start.2 = (f32[2,16,128]{2,1,0:T(8,128)S(1)}, f32[2,16,128]{2,1,0:T(8,128)S(1)}, u32[]{:S(2)}, u32[]{:S(2)}) collective-permute-start(f32[2,16,128]{2,1,0:T(8,128)S(1)} %pad_maximum_fusion.4), channel_id=1, source_target_pairs={{0,1},{1,2},{2,3},{3,4},{4,5},{5,6},{6,7},{8,9},{9,10},{10,11},{11... | collective-permute-start | bytes 49160 | tf_op jit(solution)/shard_map/ppermute | solution.py:15
  25.5 1.4 collective-permute-done.2
  26.9 0.2 fusion.19
  27.2 0.1 fusion.27
  27.3 1.3 collective-permute-start.4
  28.7 0.1 slice.325
  28.8 0.1 slice.330
  29.0 1.3 collective-permute-start.5
  30.3 0.8 collective-permute-done.4
  31.0 3.8 %collective-permute-done.5 = f32[2,16,128]{2,1,0:T(8,128)S(1)} collective-permute-done((f32[2,16,128]{2,1,0:T(8,128)S(1)}, f32[2,16,128]{2,1,0:T(8,128)S(1)}, u32[]{:S(2)}, u32[]{:S(2)}) %collective-permute-start.5) | collective-permute-done | bytes 16416 | tf_op jit(solution)/shard_map/ppermute | solution.py:15
  34.9 0.1 fusion.38
  35.1 2.5 collective-permute-start.7
  37.7 3.6 %collective-permute-start.6 = (f32[2,16,128]{2,1,0:T(8,128)S(1)}, f32[2,16,128]{2,1,0:T(8,128)S(1)}, u32[]{:S(2)}, u32[]{:S(2)}) collective-permute-start(f32[2,16,128]{2,1,0:T(8,128)S(1)} %pad_maximum_fusion.8), channel_id=1, source_target_pairs={{0,1},{1,2},{2,3},{3,4},{4,5},{5,6},{6,7},{8,9},{9,10},{10,11},{11... | collective-permute-start | bytes 49160 | tf_op jit(solution)/shard_map/ppermute | solution.py:15
  41.3 0.1 fusion.52
  41.5 1.3 collective-permute-done.6
  42.7 0.2 fusion.43
  43.0 0.0 copy-start.3
  43.0 0.3 fusion.2
  43.3 0.8 copy-done.3
  44.1 0.2 fusion
  44.3 0.8 bitcast_multiply_fusion
  45.1 0.0 all-gather.2.cloned.1.call-update
  45.1 90.5 %all-gather.2.cloned.1.call-done = f32[8,2,16,16,128]{4,3,2,1,0:T(8,128)} async-done(((f32[1,2,16,16,128]{4,3,2,1,0:T(8,128)}), f32[8,2,16,16,128]{4,3,2,1,0:T(8,128)}) %all-gather.2.cloned.1.call-update) | async-done | bytes 2097168 | tf_op jit(solution)/shard_map/all_gather | solution.py:114
  135.6 1.8 reduce_sum.31
  137.3 0.1 multiply_reduce_fusion
  137.5 134.9 %psum.7 = f32[2]{0:T(128)S(1)} all-reduce(f32[2]{0:T(128)S(1)} %multiply_reduce_fusion), channel_id=1, replica_groups=mesh['grp'=8,'gx'=8,'gy'=8] {'gx','gy'}, use_global_device_ids=true, to_apply=%region_4.5 | all-reduce | flops 2 | bytes 16 | tf_op jit(solution)/shard_map/psum | solution.py:115
  272.4 0.8 broadcast_divide_fusion
  (61 shorter events, 0.4 us)
Async XLA Ops:
  6.5 9.6 %copy-start.2 = (bf16[1,2,2,3,16,16,128]{6,5,4,3,2,1,0:T(8,128)(2,1)S(1)}, bf16[1,2,2,3,16,16,128]{6,5,4,3,2,1,0:T(8,128)(2,1)}, u32[]{:S(2)}) copy-start(bf16[1,2,2,3,16,16,128]{6,5,4,3,2,1,0:T(8,128)(2,1)} %param.13) | copy-start | bytes 2359300
  6.5 129.0 %all-gather.2.cloned.1.call-start = ((), (), s32[]{:S(2)}) async-start(), calls=%async_computation | async-start | bytes 2359296 | tf_op jit(solution)/shard_map/all_gather | solution.py:114
  7.7 8.9 %copy-start.7 = (s32[128]{0:T(128)S(1)}, s32[128]{0:T(128)}, u32[]{:S(2)}) copy-start(s32[128]{0:T(128)} %param.19) | copy-start | bytes 1540
  7.7 9.8 %collective-permute-start.1 = (f32[2,16,128]{2,1,0:T(8,128)S(1)}, f32[2,16,128]{2,1,0:T(8,128)S(1)}, u32[]{:S(2)}, u32[]{:S(2)}) collective-permute-start(f32[2,16,128]{2,1,0:T(8,128)S(1)} %pad_maximum_fusion.3), channel_id=1, source_target_pairs={{1,0},{2,1},{3,2},{4,3},{5,4},{6,5},{7,6},{9,8},{10,9},{11,10},{12... | collective-permute-start | bytes 49160 | tf_op jit(solution)/shard_map/ppermute | solution.py:15
  9.7 7.8 %collective-permute-start = (f32[2,16,128]{2,1,0:T(8,128)S(1)}, f32[2,16,128]{2,1,0:T(8,128)S(1)}, u32[]{:S(2)}, u32[]{:S(2)}) collective-permute-start(f32[2,16,128]{2,1,0:T(8,128)S(1)} %pad_maximum_fusion.2), channel_id=1, source_target_pairs={{8,0},{16,8},{24,16},{32,24},{40,32},{48,40},{56,48},{9,1},{17,9},... | collective-permute-start | bytes 49160 | tf_op jit(solution)/shard_map/ppermute | solution.py:15
  16.1 1.1 copy-start.6
  16.1 1.4 copy-start
  16.2 1.4 copy-start.4
  17.2 9.7 %copy-start.1 = (f32[16,16,128]{2,1,0:T(8,128)S(1)}, f32[16,16,128]{2,1,0:T(8,128)}, u32[]{:S(2)}) copy-start(f32[16,16,128]{2,1,0:T(8,128)} %param.14) | copy-start | bytes 393220
  17.2 9.7 %copy-start.5 = (f32[1,16,16]{2,1,0:T(8,128)S(1)}, f32[1,16,16]{2,1,0:T(8,128)}, u32[]{:S(2)}) copy-start(f32[1,16,16]{2,1,0:T(8,128)} %param.15) | copy-start | bytes 3076
  17.8 7.7 %collective-permute-start.3 = (f32[2,16,128]{2,1,0:T(8,128)S(1)}, f32[2,16,128]{2,1,0:T(8,128)S(1)}, u32[]{:S(2)}, u32[]{:S(2)}) collective-permute-start(f32[2,16,128]{2,1,0:T(8,128)S(1)} %pad_maximum_fusion.5), channel_id=1, source_target_pairs={{0,8},{8,16},{16,24},{24,32},{32,40},{40,48},{48,56},{1,9},{9,17},... | collective-permute-start | bytes 49160 | tf_op jit(solution)/shard_map/ppermute | solution.py:15
  20.9 6.0 %collective-permute-start.2 = (f32[2,16,128]{2,1,0:T(8,128)S(1)}, f32[2,16,128]{2,1,0:T(8,128)S(1)}, u32[]{:S(2)}, u32[]{:S(2)}) collective-permute-start(f32[2,16,128]{2,1,0:T(8,128)S(1)} %pad_maximum_fusion.4), channel_id=1, source_target_pairs={{0,1},{1,2},{2,3},{3,4},{4,5},{5,6},{6,7},{8,9},{9,10},{10,11},{11... | collective-permute-start | bytes 49160 | tf_op jit(solution)/shard_map/ppermute | solution.py:15
  27.3 3.7 %collective-permute-start.4 = (f32[2,16,128]{2,1,0:T(8,128)S(1)}, f32[2,16,128]{2,1,0:T(8,128)S(1)}, u32[]{:S(2)}, u32[]{:S(2)}) collective-permute-start(f32[2,16,128]{2,1,0:T(8,128)S(1)} %pad_maximum_fusion.6), channel_id=1, source_target_pairs={{8,0},{16,8},{24,16},{32,24},{40,32},{48,40},{56,48},{9,1},{17,9},... | collective-permute-start | bytes 49160 | tf_op jit(solution)/shard_map/ppermute | solution.py:15
  29.0 5.9 %collective-permute-start.5 = (f32[2,16,128]{2,1,0:T(8,128)S(1)}, f32[2,16,128]{2,1,0:T(8,128)S(1)}, u32[]{:S(2)}, u32[]{:S(2)}) collective-permute-start(f32[2,16,128]{2,1,0:T(8,128)S(1)} %pad_maximum_fusion.7), channel_id=1, source_target_pairs={{1,0},{2,1},{3,2},{4,3},{5,4},{6,5},{7,6},{9,8},{10,9},{11,10},{12... | collective-permute-start | bytes 49160 | tf_op jit(solution)/shard_map/ppermute | solution.py:15
  35.1 6.2 %collective-permute-start.7 = (f32[2,16,128]{2,1,0:T(8,128)S(1)}, f32[2,16,128]{2,1,0:T(8,128)S(1)}, u32[]{:S(2)}, u32[]{:S(2)}) collective-permute-start(f32[2,16,128]{2,1,0:T(8,128)S(1)} %pad_maximum_fusion.9), channel_id=1, source_target_pairs={{0,8},{8,16},{16,24},{24,32},{32,40},{40,48},{48,56},{1,9},{9,17},... | collective-permute-start | bytes 49160 | tf_op jit(solution)/shard_map/ppermute | solution.py:15
  37.7 5.1 %collective-permute-start.6 = (f32[2,16,128]{2,1,0:T(8,128)S(1)}, f32[2,16,128]{2,1,0:T(8,128)S(1)}, u32[]{:S(2)}, u32[]{:S(2)}) collective-permute-start(f32[2,16,128]{2,1,0:T(8,128)S(1)} %pad_maximum_fusion.8), channel_id=1, source_target_pairs={{0,1},{1,2},{2,3},{3,4},{4,5},{5,6},{6,7},{8,9},{9,10},{10,11},{11... | collective-permute-start | bytes 49160 | tf_op jit(solution)/shard_map/ppermute | solution.py:15
  43.0 1.1 copy-start.3
Sparse Core Ops, SparseCore 0:
  45.2 90.2 all-gather.1
